TPU v7x, 512 devices: a whole 4x8x8 slice. The times are simulated.
512 devices in a mesh: pair: 64 (over y, z), ctr: 8 (over x, core).
Axes of the slice: x: 4, y: 8, z: 8, core: 2. Of those that a mesh axis runs over, the one named last changes fastest.
Arguments:
- amplitudes: bfloat16 [1536, 30720], P('pair', 'ctr'), may hold values from -6 to 6
- integrals: bfloat16 [32768, 30720], P('pair', 'ctr'), may hold values from -0.03125 to 0.03125
- block_size: int32 [64], replicated, may hold values from 1 to 24, 1024 in all
- block_owner: int32 [64], replicated, may hold values from 0 to 63, each once
Outputs:
- ladder: bfloat16 [1024, 32768], P('ctr', 'pair')
Inputs may be any that keep to these rules, and one draw needn't show every extreme that they name: `block_size`: each block holds at least one occupied pair; the sizes sum to 1024 and the largest equals 24. `block_owner`: every owner holds exactly one block.
All inputs are finite; a program needn't handle non-finite values.
Results may differ from a plain program's by a relative error of at most 0.001.
Values may be sent and summed in bfloat16 or wider, within the bound.
A program may use at most 64 MiB of HBM per device.

v0:
```python
import functools

import jax
import jax.numpy as jnp
import numpy as np
from jax import lax
from jax.experimental import pallas as pl
from jax.experimental.pallas import tpu as pltpu
from jax.sharding import PartitionSpec as P

MESH = pl.DeviceIdType.MESH
NY = 8
NZ = 8
NX = 4
CAP = 24
PIECES = 3
OFFS = (0, -1, 1, -2, 2, -3, 3, -4)
GROUPS = ((0, 2), (2, 6), (6, 8))


def ring_distance(d):
    d = d % 8
    return min(d, 8 - d)


def order_tables():
    first, second, names = [], [], []
    for delta in range(8):
        order = sorted(range(8), key=lambda o: (max(ring_distance(o), ring_distance(o - delta)), o))
        done = [max(ring_distance(o), ring_distance(o - delta)) for o in order]
        assert done[1] <= 2 and done[5] <= 3
        first.append(sum(order.index(OFFS[s] % 8) * 8**s for s in range(8)))
        second.append(sum(order.index((delta + OFFS[s]) % 8) * 8**s for s in range(8)))
        names.append(sum(order[i] * 8**i for i in range(8)))
    return first, second, names


def pick(table, delta):
    total = 0
    for d in range(8):
        total = total + table[d] * (1 - lax.div(lax.rem(delta - d + 8, 8) + 7, 8))
    return total


def digit(packed, i):
    return lax.rem(lax.div(packed, 8**i), 8)


def iota(shape, dim):
    return lax.broadcasted_iota(jnp.int32, shape, dim)


def kernel(
    a_hbm, b_hbm, table_ref, out_ref,
    a_ref, msg, got, sel, blocks, b_ref, acc, early, from_core, sums, from_opposite, from_x, final,
    in_sem, b_sem, send0, recv0, send1, recv1, send2, recv2, send_c, recv_c, send_o, recv_o, send_x, recv_x,
):
    pair = lax.axis_index("pair")
    ctr = lax.axis_index("ctr")
    y, z = lax.div(pair, NZ), lax.rem(pair, NZ)
    x, core = lax.div(ctr, 2), lax.rem(ctr, 2)
    delta = lax.rem(y - z + 8, 8)
    half = a_ref.shape[1] // 2
    lane = got.shape[-1]
    piece = half // PIECES
    parts = piece // lane

    def along(axis, d):
        if axis == "y":
            return (lax.rem(y + d + NY, NY) * NZ + z, ctr)
        return (y * NZ + lax.rem(z + d + NZ, NZ), ctr)

    other_core = (pair, ctr + 1 - 2 * core)

    def along_x(d):
        return (pair, lax.rem(x + d, NX) * 2 + core)

    load_a = pltpu.make_async_copy(a_hbm, a_ref, in_sem.at[0])
    load_a.start()

    barrier = pltpu.get_barrier_semaphore()
    peers = [along("y", d) for d in range(1, 8)] + [along("z", d) for d in range(1, 8)]
    peers += [other_core] + [along_x(d) for d in (1, 2, 3)]
    for peer in peers:
        pl.semaphore_signal(barrier, inc=1, device_id=peer, device_id_type=MESH)

    sends = []

    def send(src, dst, send_sem, recv_sem, device):
        copy = pltpu.make_async_remote_copy(
            src_ref=src, dst_ref=dst, send_sem=send_sem, recv_sem=recv_sem,
            device_id=device, device_id_type=MESH,
        )
        copy.start()
        sends.append(copy)
        return copy

    def drain(count):
        for copy in sends[:count]:
            copy.wait_send()
        del sends[:count]

    size_row = (table_ref[...] >> 6).astype(jnp.float32)
    owner_row = (table_ref[...] & 63).astype(jnp.float32)
    n_block = size_row.shape[1]
    rows, cols = iota((n_block, n_block), 0), iota((n_block, n_block), 1)
    zero = jnp.zeros((n_block, n_block), jnp.float32)
    size_col = jnp.sum(jnp.where(rows == cols, size_row + zero, 0.0), axis=1, keepdims=True)
    owner_col = jnp.sum(jnp.where(rows == cols, owner_row + zero, 0.0), axis=1, keepdims=True)
    offset_col = jnp.sum(jnp.where(cols < rows, size_row + zero, 0.0), axis=1, keepdims=True)

    mine = owner_col == pair.astype(jnp.float32)
    my_offset = jnp.sum(jnp.where(mine, offset_col, 0.0), axis=0, keepdims=True).astype(jnp.int32)
    n_msg = 8 * 16
    at = iota((n_msg, CAP), 0)
    slot = iota((n_msg, CAP), 1)
    wanted = jnp.where(
        ((slot + my_offset) & 7) == (at >> 4), (at & 15) - parts * (slot >> 3), -1
    )
    choose = [jnp.where(wanted == q, 1.0, 0.0).astype(jnp.bfloat16) for q in range(parts)]
    load_a.wait()
    loads = []
    for h in range(2):
        load = pltpu.make_async_copy(b_hbm.at[:, pl.ds(h * half, half)], b_ref.at[h], b_sem.at[h])
        load.start()
        loads.append(load)

    for h in range(2):
        for a in range(PIECES):
            total = jnp.zeros((n_msg, lane), jnp.float32)
            for q in range(parts):
                start = h * half + a * piece + q * lane
                total += jnp.dot(
                    choose[q], a_ref[:, start : start + lane], preferred_element_type=jnp.float32
                )
            msg[h, a] = total.astype(jnp.bfloat16).reshape(8, 16, lane)

    pl.semaphore_wait(barrier, len(peers))

    phase0 = []
    for d in (4, 3, 5, 2, 6, 1, 7):
        for h, axis, me in ((0, "z", z), (1, "y", y)):
            phase0.append(
                send(
                    msg.at[h, :, lax.rem(me + d, 8)], got.at[h, :, 0, me],
                    send0.at[h, d - 1], recv0.at[h, d - 1], along(axis, d),
                )
            )
    for a in range(PIECES):
        got[0, a, 0, z] = msg[0, a, z]
        got[1, a, 0, y] = msg[1, a, y]

    width = got.shape[2] * n_msg
    place = iota((1, width), 1)
    slot_of = place >> 7
    source = (place >> 4) & 7
    m = place & 15
    i = jnp.where(m >= parts, 1, 0) + jnp.where(m >= 2 * parts, 1, 0) + jnp.where(m >= 3 * parts, 1, 0)
    q = m - parts * i
    step = (slot_of + 1) >> 1
    ring = jnp.where((slot_of & 1) == 0, step, 8 - step)

    targets = []
    for h in range(2):
        if h == 0:
            owner = ((ring + y) & 7) * NZ + source
            cls = z
        else:
            owner = source * NZ + ((ring + z) & 7)
            cls = y
        hit = owner_col == owner.astype(jnp.float32)
        first = jnp.sum(jnp.where(hit, offset_col, 0.0), axis=0, keepdims=True).astype(jnp.int32)
        count = jnp.sum(jnp.where(hit, size_col, 0.0), axis=0, keepdims=True).astype(jnp.int32)
        k = ((first - cls + 7) >> 3) + i
        good = (8 * k + cls < first + count) & (i < 3)
        target = q * 128 + ((k >> 4) & 1) * 64 + (k >> 5) * 16 + (k & 15)
        targets.append(jnp.where(good, target, -1))

    def select(h):
        def fill(part, carry):
            row = iota((128, width), 0) + part * 128
            sel[h, pl.ds(part * 128, 128)] = jnp.where(row == targets[h], 1.0, 0.0).astype(jnp.bfloat16)
            return carry

        lax.fori_loop(0, parts, fill, 0)

    for copy in phase0:
        copy.wait_recv()

    lanes = (("y", "z"), ("z", "y"))

    def ring_send(view, n_rows, h, a, way, step, send_sem, recv_sem, axis):
        src = 0 if step == 0 else 2 * step - 1 + way
        dst = 7 if step == 3 else 2 * step + 1 + way
        rows = pl.ds(0, n_rows) if step < 3 else pl.ds(way * (n_rows // 2), n_rows // 2)
        return send(
            view(h, a, src, rows), view(h, a, dst, rows),
            send_sem.at[h, way, step, a], recv_sem.at[h, way, step, a],
            along(axis, 1 if way == 0 else -1),
        )

    flying1, flying2 = {}, {}

    def first_ring(step, a, h, way):
        flying1[step, a, h, way] = ring_send(
            lambda h, a, slot, rows: got.at[h, a, slot, rows], 8,
            h, a, way, step, send1, recv1, lanes[h][0],
        )

    def second_ring(step, a, h, way):
        flying2[step, a, h, way] = ring_send(
            lambda h, a, slot, rows: blocks.at[h, slot, rows, pl.ds(a * piece, piece)], 128,
            h, a, way, step, send2, recv2, lanes[h][1],
        )

    both = [(h, way) for way in range(2) for h in range(2)]
    for a in range(PIECES):
        for h, way in both:
            first_ring(0, a, h, way)
    select(0)
    acc[...] = jnp.zeros_like(acc)
    for step in range(3):
        for a in range(PIECES):
            for h, way in both:
                flying1[step, a, h, way].wait_recv()
                first_ring(step + 1, a, h, way)
            if step == 2 and a == 0:
                for h in range(2):
                    early[h] += jnp.dot(
                        sel[h, :, 5 * n_msg : 7 * n_msg], got[h, 0, 5:7].reshape(2 * n_msg, lane),
                        preferred_element_type=jnp.float32,
                    )
        if step == 0:
            select(1)
        if step == 1:
            for h in range(2):
                early[h] = jnp.dot(
                    sel[h, :, : 5 * n_msg], got[h, 0, :5].reshape(5 * n_msg, lane),
                    preferred_element_type=jnp.float32,
                )

    n_early = len(sends)

    for a in range(PIECES):
        for h in range(2):
            for way in range(2):
                flying1[3, a, h, way].wait_recv()
            if a == 0:
                value = early[h] + jnp.dot(
                    sel[h, :, 7 * n_msg :], got[h, 0, 7].reshape(n_msg, lane),
                    preferred_element_type=jnp.float32,
                )
            else:
                value = jnp.dot(
                    sel[h], got[h, a].reshape(width, lane), preferred_element_type=jnp.float32
                )
            value = value.astype(jnp.bfloat16)
            for q in range(parts):
                start = a * piece + q * lane
                blocks[h, 0, :, start : start + lane] = value[q * 128 : q * 128 + 128]
            for way in range(2):
                second_ring(0, a, h, way)

    first_table, second_table, name_table = order_tables()
    where_to = (pick(first_table, delta), pick(second_table, delta))
    names = pick(name_table, delta)

    def multiply(slot0, n_slot, a):
        for h in range(2):
            columns = pl.ds(a * piece, piece)
            left = blocks[h, slot0 : slot0 + n_slot, :, columns].reshape(n_slot * 128, piece)
            value = lax.dot_general(
                left, b_ref[h, :, columns], (((1,), (1,)), ((), ())), preferred_element_type=jnp.float32
            )
            for s in range(n_slot):
                pos = digit(where_to[h], slot0 + s)
                for c in range(2):
                    acc[c, pos] += value[s * 128 + c * 64 : s * 128 + c * 64 + 64]

    def arrive(step, a):
        for h, way in both:
            flying2[step, a, h, way].wait_recv()
            if step < 3:
                second_ring(step + 1, a, h, way)

    def core_send(g):
        lo, hi = GROUPS[g]
        return send(
            acc.at[1 - core, pl.ds(lo, hi - lo)], from_core.at[pl.ds(lo, hi - lo)],
            send_c.at[g], recv_c.at[g], other_core,
        )

    right, left, opposite = (lax.rem(x + d, NX) for d in (1, 3, 2))

    def add_cores(g, exchanged):
        lo, hi = GROUPS[g]
        exchanged.wait_recv()
        for t in range(NX):
            sums[t, lo:hi] = acc[core, lo:hi, t * 16 : t * 16 + 16] + from_core[lo:hi, t * 16 : t * 16 + 16]

    def x_direct(g, exchanged):
        lo, hi = GROUPS[g]
        add_cores(g, exchanged)
        return [
            send(
                sums.at[lax.rem(x + d, NX), pl.ds(lo, hi - lo)], from_x.at[w, pl.ds(lo, hi - lo)],
                send_x.at[g, w], recv_x.at[g, w], along_x(d),
            )
            for w, d in ((2, 2), (0, 1), (1, 3))
        ]

    def x_first(g, exchanged):
        lo, hi = GROUPS[g]
        add_cores(g, exchanged)
        return [
            send(
                sums.at[opposite, pl.ds(lo, hi - lo), pl.ds(w * 8, 8)], from_opposite.at[w, pl.ds(lo, hi - lo)],
                send_o.at[g, w], recv_o.at[g, w], along_x((1, 3)[w]),
            )
            for w in range(2)
        ]

    def x_second(g, copies):
        lo, hi = GROUPS[g]
        out = []
        for w, near in ((0, right), (1, left)):
            copies[w].wait_recv()
            sums[near, lo:hi, w * 8 : w * 8 + 8] += from_opposite[w, lo:hi]
            out.append(
                send(
                    sums.at[near, pl.ds(lo, hi - lo)], from_x.at[w, pl.ds(lo, hi - lo)],
                    send_x.at[g, w], recv_x.at[g, w], along_x((1, 3)[w]),
                )
            )
        return out

    def finish(g, copies):
        lo, hi = GROUPS[g]
        for copy in copies:
            copy.wait_recv()
        value = sums[x, lo:hi] + from_x[0, lo:hi] + from_x[1, lo:hi]
        if len(copies) == 3:
            value += from_x[2, lo:hi]
        final[lo:hi] = value.astype(jnp.bfloat16)

    for load in loads:
        load.wait()
    for a in range(PIECES):
        multiply(0, 1, a)
    for step in range(2):
        for a in range(PIECES):
            arrive(step, a)
            multiply(2 * step + 1, 2, a)
            if step == 0 and a == 0:
                drain(n_early)
    core_a = core_send(0)
    n_early = len(sends)
    for a in range(PIECES):
        arrive(2, a)
        if a == 0:
            x_a = x_first(0, core_a)
        multiply(5, 2, a)
        if a == 1:
            x_a = x_second(0, x_a)
    core_b = core_send(1)
    row, col = iota((128, 128), 0), iota((128, 128), 1)
    pos = col >> 4
    cls = jnp.zeros((128, 128), jnp.int32)
    for n in range(8):
        cls = jnp.where(pos == n, lax.rem(digit(names, n) + z, 8), cls)
    order = jnp.where(row == (col & 15) * 8 + cls, 1.0, 0.0).astype(jnp.bfloat16)
    for a in range(PIECES):
        arrive(3, a)
        if a == 0:
            x_b = x_first(1, core_b)
        multiply(7, 1, a)
        if a == 1:
            x_b = x_second(1, x_b)
            drain(n_early)
            finish(0, x_a)
    core_c = core_send(2)
    x_c = x_direct(2, core_c)
    finish(1, x_b)
    drain(len(sends) - 3)
    finish(2, x_c)
    value = jnp.dot(order, final[...].reshape(128, final.shape[-1]), preferred_element_type=jnp.float32)
    out_ref[...] = value.astype(jnp.bfloat16)
    drain(len(sends))


def on_device(amplitudes, integrals, block_size, block_owner):
    slots, depth = amplitudes.shape
    ab = integrals.shape[0]
    half = depth // 2
    lane = half // PIECES // 5
    n_blocks = block_size.shape[0]
    vmem = pl.BlockSpec(memory_space=pltpu.VMEM)
    dma = pltpu.SemaphoreType.DMA
    return pl.pallas_call(
        kernel,
        out_shape=jax.ShapeDtypeStruct((128, ab), jnp.bfloat16),
        in_specs=[pl.BlockSpec(memory_space=pltpu.HBM)] * 2 + [vmem],
        out_specs=vmem,
        scratch_shapes=[
            pltpu.VMEM((slots, depth), jnp.bfloat16),
            pltpu.VMEM((2, PIECES, 8, 16, lane), jnp.bfloat16),
            pltpu.VMEM((2, PIECES, 8, 8, 16, lane), jnp.bfloat16),
            pltpu.VMEM((2, 5 * 128, 8 * 128), jnp.bfloat16),
            pltpu.VMEM((2, 8, 128, half), jnp.bfloat16),
            pltpu.VMEM((2, ab, half), jnp.bfloat16),
            pltpu.VMEM((2, 8, 64, ab), jnp.float32),
            pltpu.VMEM((2, 5 * 128, lane), jnp.float32),
            pltpu.VMEM((8, 64, ab), jnp.float32),
            pltpu.VMEM((NX, 8, 16, ab), jnp.float32),
            pltpu.VMEM((2, 8, 8, ab), jnp.float32),
            pltpu.VMEM((3, 8, 16, ab), jnp.float32),
            pltpu.VMEM((8, 16, ab), jnp.bfloat16),
            dma((1,)),
            dma((2,)),
            dma((2, 7)),
            dma((2, 7)),
            dma((2, 2, 4, PIECES)),
            dma((2, 2, 4, PIECES)),
            dma((2, 2, 4, PIECES)),
            dma((2, 2, 4, PIECES)),
            dma((3,)),
            dma((3,)),
            dma((3, 2)),
            dma((3, 2)),
            dma((3, 3)),
            dma((3, 3)),
        ],
        compiler_params=pltpu.CompilerParams(
            collective_id=0, has_side_effects=True, vmem_limit_bytes=55040 * 1024
        ),
        cost_estimate=pl.CostEstimate(
            flops=2 * 1024 * ab * depth, bytes_accessed=2 * ab * depth, transcendentals=0
        ),
    )(
        amplitudes,
        integrals,
        (block_size * 64 + block_owner).reshape(1, n_blocks),
    )


def solution(mesh):
    in_specs = (P("pair", "ctr"), P("pair", "ctr"), P(), P())
    return jax.shard_map(
        on_device, mesh=mesh, in_specs=in_specs, out_specs=P("ctr", "pair"), check_vma=False
    )
```

profile of v0, /device:TPU:1, one launch (start us, length us, event | category | flops | bytes accessed | tf_op | source)
XLA Modules:
  0.0 84.8 jit_solution(13225272786114927641)
XLA Ops:
  0.0 0.7 add_bitcast_fusion.table_ref
  0.7 83.5 %shard_map.46 = bf16[128,512]{1,0:T(8,128)(2,1)S(1)} custom-call(bf16[24,3840]{1,0:T(8,128)(2,1)} %a_hbm.1, bf16[512,3840]{1,0:T(8,128)(2,1)} %b_hbm.1, s32[1,64]{1,0:T(1,128)S(1)} %add_bitcast_fusion.table_ref), custom_call_target="tpu_custom_call" | custom-call | flops 4026531840 | bytes 3932160 | tf_op jit(solution)/shard_map/pallas_call | solution.py:399
  84.2 0.7 copy.6
where the time goes:
time: 85 us; the launch traced here: 84.8 us
  Pallas kernels  83.5 us (98%)
    pallas_call x1, Pallas kernels, on_device(): pl.pallas_call(kernel, out_shape=jax.ShapeDtypeStruct((128, ab), jnp.bflo...  83.5 us

commit v1 on v0

--- a/solution.py
+++ b/solution.py
@@ -265,8 +265,8 @@
     where_to = (pick(first_table, delta), pick(second_table, delta))
     names = pick(name_table, delta)
 
-    def multiply(slot0, n_slot, a):
-        for h in range(2):
+    def multiply(slot0, n_slot, a, halves=(0, 1)):
+        for h in halves:
             columns = pl.ds(a * piece, piece)
             left = blocks[h, slot0 : slot0 + n_slot, :, columns].reshape(n_slot * 128, piece)
             value = lax.dot_general(
@@ -285,16 +285,20 @@
 
     def core_send(g):
         lo, hi = GROUPS[g]
+        return [core_send_at(g, lo, hi - lo)]
+
+    def core_send_at(n, pos, count):
         return send(
-            acc.at[1 - core, pl.ds(lo, hi - lo)], from_core.at[pl.ds(lo, hi - lo)],
-            send_c.at[g], recv_c.at[g], other_core,
+            acc.at[1 - core, pl.ds(pos, count)], from_core.at[pl.ds(pos, count)],
+            send_c.at[n], recv_c.at[n], other_core,
         )
 
     right, left, opposite = (lax.rem(x + d, NX) for d in (1, 3, 2))
 
     def add_cores(g, exchanged):
         lo, hi = GROUPS[g]
-        exchanged.wait_recv()
+        for copy in exchanged:
+            copy.wait_recv()
         for t in range(NX):
             sums[t, lo:hi] = acc[core, lo:hi, t * 16 : t * 16 + 16] + from_core[lo:hi, t * 16 : t * 16 + 16]
 
@@ -358,10 +362,8 @@
     for a in range(PIECES):
         arrive(2, a)
         if a == 0:
-            x_a = x_first(0, core_a)
+            x_a = x_direct(0, core_a)
         multiply(5, 2, a)
-        if a == 1:
-            x_a = x_second(0, x_a)
     core_b = core_send(1)
     row, col = iota((128, 128), 0), iota((128, 128), 1)
     pos = col >> 4
@@ -373,12 +375,17 @@
         arrive(3, a)
         if a == 0:
             x_b = x_first(1, core_b)
-        multiply(7, 1, a)
+        if a < 2:
+            multiply(7, 1, a)
         if a == 1:
             x_b = x_second(1, x_b)
             drain(n_early)
             finish(0, x_a)
-    core_c = core_send(2)
+    last = digit(where_to[1], 7)
+    multiply(7, 1, 2, (0,))
+    core_c = [core_send_at(2, 13 - last, 1)]
+    multiply(7, 1, 2, (1,))
+    core_c += [core_send_at(3, last, 1)]
     x_c = x_direct(2, core_c)
     finish(1, x_b)
     drain(len(sends) - 3)
@@ -423,8 +430,8 @@
             dma((2, 2, 4, PIECES)),
             dma((2, 2, 4, PIECES)),
             dma((2, 2, 4, PIECES)),
-            dma((3,)),
-            dma((3,)),
+            dma((4,)),
+            dma((4,)),
             dma((3, 2)),
             dma((3, 2)),
             dma((3, 3)),

time: 85 us -> 85 us (level)
  no operation moved by 1% of the time
where the time goes in v1:
time: 85 us; the launch traced here: 84.8 us
  Pallas kernels  83.5 us (98%)
    pallas_call x1, Pallas kernels, on_device(): pl.pallas_call(kernel, out_shape=jax.ShapeDtypeStruct((128, ab), jnp.bflo...  83.5 us

profile of v1, /device:TPU:1, one launch (start us, length us, event | category | flops | bytes accessed | tf_op | source)
XLA Modules:
  0.0 84.8 jit_solution(9082658668164193801)
XLA Ops:
  0.0 0.7 add_bitcast_fusion.table_ref
  0.7 83.5 %shard_map.46 = bf16[128,512]{1,0:T(8,128)(2,1)S(1)} custom-call(bf16[24,3840]{1,0:T(8,128)(2,1)} %a_hbm.1, bf16[512,3840]{1,0:T(8,128)(2,1)} %b_hbm.1, s32[1,64]{1,0:T(1,128)S(1)} %add_bitcast_fusion.table_ref), custom_call_target="tpu_custom_call" | custom-call | flops 4026531840 | bytes 3932160 | tf_op jit(solution)/shard_map/pallas_call | solution.py:406
  84.2 0.7 copy.6
